TPU v7x, 32 devices: a whole 2x2x4 slice. The times are simulated.
32 devices in a mesh: dp: 8 (over z, core), zero: 4 (over y, x).
Axes of the slice: x: 2, y: 2, z: 4, core: 2. Of those that a mesh axis runs over, the one named last changes fastest.
Arguments:
- pre_acts: bfloat16 [4096, 2560], P(('dp', 'zero')), may hold values from -6 to 6
- cotangent: bfloat16 [4096, 640], P(('dp', 'zero')), may hold values from -6 to 6
- w_out: bfloat16 [1280, 640], P('zero'), may hold values from -0.25 to 0.25
Outputs:
- d_pre: bfloat16 [4096, 2560], P(('dp', 'zero'))
- d_w: float32 [4, 204800], P('zero', 'dp')
All inputs are finite; a program needn't handle non-finite values.
Results may differ from a plain program's by a relative error of at most 0.0028.
Values may be sent and summed in bfloat16 or wider, within the bound.
A program may use at most 64 MiB of HBM per device.

v0:
```python
import math

import jax
import jax.numpy as jnp
from jax import lax
from jax.sharding import PartitionSpec as P

D = 640
FFH = 1280


def body(pre_acts, cotangent, w_out):
    n_zero = lax.axis_size("zero")
    n_data = lax.axis_size("dp")
    tokens_all = pre_acts.shape[0] * n_data * n_zero
    scale = 1.0 / math.sqrt(tokens_all)
    value = pre_acts[:, :FFH].astype(jnp.float32)
    gate = pre_acts[:, FFH:].astype(jnp.float32)
    cdf = 0.5 * (1.0 + jax.scipy.special.erf(gate / math.sqrt(2.0)))
    act = gate * cdf
    hidden = (value * act).astype(jnp.bfloat16)
    d_hidden = jnp.einsum(
        "td,hd->th",
        cotangent,
        lax.all_gather(w_out, "zero", axis=0, tiled=True),
        preferred_element_type=jnp.float32,
    )
    dens = jnp.exp(-0.5 * gate * gate) / math.sqrt(2.0 * math.pi)
    d_value = d_hidden * act
    d_gate = d_hidden * value * (cdf + gate * dens)
    d_pre = jnp.concatenate([d_value, d_gate], axis=1).astype(jnp.bfloat16)
    own_rows = FFH // n_zero
    flat_len = own_rows * D
    piece_len = flat_len // n_data
    owned = lax.psum_scatter(
        jnp.einsum("th,td->hd", hidden, cotangent, preferred_element_type=jnp.float32) * scale,
        "zero",
        scatter_dimension=0,
        tiled=True,
    )
    blocks = owned.reshape(n_data, piece_len)
    d_w = lax.psum_scatter(blocks, "dp", scatter_dimension=0, tiled=True)
    return (d_pre, d_w)


def solution(mesh):
    return jax.shard_map(
        body,
        mesh=mesh,
        in_specs=(P(("dp", "zero"), None), P(("dp", "zero"), None), P("zero", None)),
        out_specs=(P(("dp", "zero"), None), P("zero", "dp")),
        check_vma=False,
    )
```

profile of v0, /device:TPU:1, one launch (start us, length us, event | category | flops | bytes accessed | tf_op | source)
XLA Modules:
  0.0 159.8 jit_solution(14616411293383875002)
XLA Ops:
  7.2 0.0 copy-start
  7.2 0.0 reduce-scatter.2.cloned.1.call-start
  7.2 0.9 copy-done
  8.1 3.4 %convolution_multiply_fusion = f32[1280,640]{1,0:T(8,128)} fusion(bf16[128,640]{1,0:T(8,128)(2,1)S(1)} %copy-done, bf16[128,2560]{1,0:T(8,128)(2,1)} %param.3), kind=kOutput, calls=%fused_computation | convolution fusion | flops 211845120 | bytes 4096000 | tf_op jit(solution)/shard_map/th,td->hd/dot_general | solution.py:36
  11.5 0.0 copy-start.2
  11.5 0.0 reduce-scatter.2.cloned.1.call-update
  11.5 0.0 copy-start.1
  11.5 0.0 all-gather.2.cloned.1.call-start
  11.6 0.7 all-gather.2.cloned.1.call-update
  12.3 0.0 all-reduce.3.cloned.1.call-start
  12.3 0.0 copy-done.2
  12.3 0.7 dynamic-slice
  13.0 45.8 %reduce-scatter.2.cloned.1.call-done = f32[320,640]{1,0:T(8,128)} async-done(((f32[1280,640]{1,0:T(8,128)}), f32[320,640]{1,0:T(8,128)}) %reduce-scatter.2.cloned.1.call-update) | async-done | bytes 819216 | tf_op jit(solution)/shard_map/reduce_scatter | solution.py:35
  58.8 2.2 %reshape.7 = f32[8,25600]{1,0:T(8,128)} reshape(f32[320,640]{1,0:T(8,128)} %reduce-scatter.2.cloned.1.call-done) | data formatting | bytes 1638400 | tf_op jit(solution)/shard_map/reshape | solution.py:41
  61.0 0.0 all-reduce.3.cloned.1.call-update
  61.0 31.2 %all-gather.2.cloned.1.call-done = bf16[1280,640]{1,0:T(8,128)(2,1)} async-done(((bf16[320,640]{1,0:T(8,128)(2,1)}), bf16[1280,640]{1,0:T(8,128)(2,1)}) %all-gather.2.cloned.1.call-update) | async-done | bytes 1638416 | tf_op jit(solution)/shard_map/all_gather | solution.py:25
  92.2 0.0 copy-done.1
  92.2 2.1 %multiply_convert_fusion = (bf16[128,1280]{1,0:T(8,128)(2,1)S(1)}, bf16[128,1280]{1,0:T(8,128)(2,1)S(1)}) fusion(bf16[128,2560]{1,0:T(8,128)(2,1)S(1)} %copy-done.1, bf16[128,640]{1,0:T(8,128)(2,1)S(1)} %copy-done, bf16[1280,640]{1,0:T(8,128)(2,1)} %all-gather.2.cloned.1.call-done), kind=kOutput, calls=%fused_computation.18 | convolution fusion | flops 212336640 | bytes 3112960 | tf_op jit(solution)/shard_map/td,hd->th/dot_general | solution.py:22
  94.3 0.9 pad_maximum_fusion
  95.2 55.5 %all-reduce.3.cloned.1.call-done = f32[8,25600]{1,0:T(8,128)} async-done(((f32[8,25600]{1,0:T(8,128)}), f32[8,25600]{1,0:T(8,128)}) %all-reduce.3.cloned.1.call-update) | async-done | bytes 819216
  150.7 2.5 %constant_dynamic-slice_fusion = f32[1,25600]{1,0:T(1,128)} fusion(f32[8,25600]{1,0:T(8,128)} %all-reduce.3.cloned.1.call-done, u32[]{:T(128)} %bitcast), kind=kLoop, calls=%fused_computation.21 | loop fusion | bytes 204804
Async XLA Ops:
  7.2 0.9 copy-start
  7.2 51.7 %reduce-scatter.2.cloned.1.call-start = ((), (), s32[]{:S(2)}) async-start(), calls=%async_computation.2 | async-start | bytes 4096000 | tf_op jit(solution)/shard_map/reduce_scatter | solution.py:35
  11.5 0.8 copy-start.2
  11.5 80.7 %copy-start.1 = (bf16[128,2560]{1,0:T(8,128)(2,1)S(1)}, bf16[128,2560]{1,0:T(8,128)(2,1)}, u32[]{:S(2)}) copy-start(bf16[128,2560]{1,0:T(8,128)(2,1)} %param.3) | copy-start | bytes 1966084
  11.5 80.7 %all-gather.2.cloned.1.call-start = ((), (), s32[]{:S(2)}) async-start(), calls=%async_computation.1 | async-start | bytes 2048000 | tf_op jit(solution)/shard_map/all_gather | solution.py:25
  12.3 138.4 %all-reduce.3.cloned.1.call-start = ((), (), s32[]{:S(2)}) async-start(), calls=%async_computation.3 | async-start | bytes 1638400
Sparse Core Ops, SparseCore 0:
  11.6 47.1 reduce-scatter.1
  60.7 31.4 all-gather.1
  94.6 56.0 all-reduce.2
where the time goes:
time: 162 us; the launch traced here: 160 us
  waiting for transfers between devices  133 us (82%)
  between operations  13.8 us (9%)
  local copies, waits for them, and re-layouts  6.28 us (4%)
  matrix products  5.49 us (3%)
    unnamed x4, waiting for transfers between devices  56.2 us
    reduce_scatter x1, waiting for transfers between devices, body(): lax.psum_scatter(jnp.einsum('th,td->hd', hidden, cotangent, preferred_ele...  45.8 us
    all_gather x1, waiting for transfers between devices, body(): lax.all_gather(w_out, 'zero', axis=0, tiled=True)  31.2 us
    unnamed x8, local copies, waits for them, and re-layouts  4.09 us
    dot_general x1, matrix products, body(): jnp.einsum('th,td->hd', hidden, cotangent, preferred_element_type=jnp.flo...  3.41 us
  transfers between devices with their start and end apart: 3, of which 3 were waited for; matrix products, arithmetic and copies ran while one was open for 4% of the time, Pallas kernels for 0%

commit v1 on v0

v1 whole, which is shorter than its diff:
```python
import functools
import math

import jax
import jax.numpy as jnp
from jax import lax
from jax.experimental import pallas as pl
from jax.experimental.pallas import tpu as pltpu
from jax.sharding import PartitionSpec as P

LANES = 128
MESH = pl.DeviceIdType.MESH


def gate_parts(gate):
    cdf = 0.5 * (1.0 + lax.erf(gate / math.sqrt(2.0)))
    dens = jnp.exp(-0.5 * gate * gate) / math.sqrt(2.0 * math.pi)
    return gate * cdf, cdf + gate * dens


def general_body(pre_acts, cotangent, w_out):
    n_zero = lax.axis_size("zero")
    n_data = lax.axis_size("dp")
    width = cotangent.shape[1]
    ffh = pre_acts.shape[1] // 2
    scale = 1.0 / math.sqrt(pre_acts.shape[0] * n_data * n_zero)
    value = pre_acts[:, :ffh].astype(jnp.float32)
    gate = pre_acts[:, ffh:].astype(jnp.float32)
    act, slope = gate_parts(gate)
    hidden = (value * act).astype(jnp.bfloat16)
    d_hidden = jnp.einsum(
        "td,hd->th",
        cotangent,
        lax.all_gather(w_out, "zero", axis=0, tiled=True),
        preferred_element_type=jnp.float32,
    )
    d_pre = jnp.concatenate([d_hidden * act, d_hidden * value * slope], axis=1)
    d_pre = d_pre.astype(jnp.bfloat16)
    owned = lax.psum_scatter(
        jnp.einsum("th,td->hd", hidden, cotangent, preferred_element_type=jnp.float32) * scale,
        "zero",
        scatter_dimension=0,
        tiled=True,
    )
    blocks = owned.reshape(n_data, ffh // n_zero * width // n_data)
    d_w = lax.psum_scatter(blocks, "dp", scatter_dimension=0, tiled=True)
    return (d_pre, d_w)


def kernel(
    n_zero, n_data, scale,
    pre_hbm, cot_hbm, w_hbm,
    d_pre, d_w,
    pre, cot_all, w_all, act_s, slope_s, hid_t, hid_all, grad, grad_in, part, part_in,
    local_sem, cot_send, cot_recv, hid_send, hid_recv, w_send, w_recv,
    relay_send, relay_recv, pair_send, pair_recv, z_send, z_recv,
):
    tokens, width = cot_hbm.shape
    own_rows = w_hbm.shape[0]
    ffh = own_rows * n_zero
    half = own_rows // 2
    n_z = n_data // 2
    piece = own_rows // n_data
    cols = width // LANES
    zero = lax.axis_index("zero")
    dp = lax.axis_index("dp")
    core = lax.rem(dp, 2)
    z = lax.div(dp, 2)
    twin = z * 2 + (1 - core)

    def zero_at(step):
        return lax.rem(zero + step, n_zero)

    def z_at(step):
        return lax.rem(z + step, n_z)

    def rows(index, size):
        return pl.ds(pl.multiple_of(index * size, size), size)

    into = [
        pltpu.make_async_copy(cot_hbm, cot_all.at[zero], local_sem.at[0]),
        pltpu.make_async_copy(pre_hbm, pre, local_sem.at[1]),
        pltpu.make_async_copy(w_hbm, w_all.at[rows(zero, own_rows), :], local_sem.at[2]),
    ]
    for copy in into:
        copy.start()

    barrier = pltpu.get_barrier_semaphore()
    for step in range(1, n_zero):
        pl.semaphore_signal(barrier, inc=1, device_id=(dp, zero_at(step)), device_id_type=MESH)
    for step in range(1, n_z):
        pl.semaphore_signal(
            barrier, inc=1, device_id=(z_at(step) * 2 + core, zero), device_id_type=MESH
        )
    pl.semaphore_signal(barrier, inc=1, device_id=(twin, zero), device_id_type=MESH)
    pl.semaphore_wait(barrier, n_zero - 1 + n_z - 1 + 1)

    cots = []
    for step in range(1, n_zero):
        cots.append(pltpu.make_async_remote_copy(
            src_ref=cot_hbm, dst_ref=cot_all.at[zero],
            send_sem=cot_send.at[step], recv_sem=cot_recv.at[step],
            device_id=(dp, zero_at(step)), device_id_type=MESH,
        ))
        cots[-1].start()

    into[1].wait()
    for tile in range(ffh // LANES):
        at = pl.ds(tile * LANES, LANES)
        value = pre[:, at].astype(jnp.float32)
        gate = pre[:, pl.ds(ffh + tile * LANES, LANES)].astype(jnp.float32)
        act, slope = gate_parts(gate)
        act_s[:, at] = act
        slope_s[:, at] = value * slope
        hid_t[at, :] = (value * act).T.astype(jnp.bfloat16)
    hids = []
    for step in range(1, n_zero):
        hids.append(pltpu.make_async_remote_copy(
            src_ref=hid_t.at[rows(zero_at(step), own_rows), :], dst_ref=hid_all.at[zero],
            send_sem=hid_send.at[step], recv_sem=hid_recv.at[step],
            device_id=(dp, zero_at(step)), device_id_type=MESH,
        ))
        hids[-1].start()

    def w_half(block, part_of):
        return pl.ds(pl.multiple_of(block * own_rows + part_of * half, half), half)

    ws = []
    for step in range(1, n_zero):
        ws.append(pltpu.make_async_remote_copy(
            src_ref=w_hbm.at[w_half(0, core), :], dst_ref=w_all.at[w_half(zero, core), :],
            send_sem=w_send.at[step], recv_sem=w_recv.at[step],
            device_id=(dp, zero_at(step)), device_id_type=MESH,
        ))
        ws[-1].start()

    into[0].wait()
    grad[...] = jnp.dot(
        hid_t[rows(zero, own_rows), :], cot_all[zero], preferred_element_type=jnp.float32
    ).reshape(grad.shape)
    for step in range(1, n_zero):
        source = lax.rem(zero + n_zero - step, n_zero)
        cots[step - 1].wait_recv()
        hids[step - 1].wait_recv()
        grad[...] += jnp.dot(
            hid_all[source], cot_all[source], preferred_element_type=jnp.float32
        ).reshape(grad.shape)

    pairs = []
    for k in range(n_z):
        pairs.append(pltpu.make_async_remote_copy(
            src_ref=grad.at[k * 2 + (1 - core)], dst_ref=grad_in.at[k],
            send_sem=pair_send.at[k], recv_sem=pair_recv.at[k],
            device_id=(twin, zero), device_id_type=MESH,
        ))
        pairs[-1].start()

    relays = []
    for step in range(1, n_zero):
        source = lax.rem(zero + n_zero - step, n_zero)
        relays.append(pltpu.make_async_remote_copy(
            src_ref=w_all.at[w_half(source, core), :], dst_ref=w_all.at[w_half(source, core), :],
            send_sem=relay_send.at[step], recv_sem=relay_recv.at[step],
            device_id=(twin, zero), device_id_type=MESH,
        ))

    for k in range(n_z):
        pairs[k].wait_recv()
    pad = part.shape[1] - cols * piece
    sends = []
    for step in range(1, n_z):
        owner = z_at(step)
        total = (grad[owner * 2 + core] + grad_in[owner]) * scale
        tall = [total[:, i * LANES:(i + 1) * LANES] for i in range(cols)]
        if pad:
            tall.append(jnp.zeros((pad, LANES), jnp.float32))
        part[step] = jnp.concatenate(tall, axis=0).astype(jnp.bfloat16)
        sends.append(pltpu.make_async_remote_copy(
            src_ref=part.at[step], dst_ref=part_in.at[step],
            send_sem=z_send.at[step], recv_sem=z_recv.at[step],
            device_id=(owner * 2 + core, zero), device_id_type=MESH,
        ))
        sends[-1].start()

    for step in range(1, n_zero):
        ws[step - 1].wait_recv()
        relays[step - 1].start()

    into[2].wait()
    for step in range(1, n_zero):
        relays[step - 1].wait_recv()
    cot = cot_all[zero]
    for tile in range(ffh // (2 * LANES)):
        at = pl.ds(tile * 2 * LANES, 2 * LANES)
        d_hidden = lax.dot_general(
            cot, w_all[at, :], (((1,), (1,)), ((), ())), preferred_element_type=jnp.float32
        )
        d_pre[:, at] = (d_hidden * act_s[:, at]).astype(jnp.bfloat16)
        d_pre[:, pl.ds(ffh + tile * 2 * LANES, 2 * LANES)] = (
            d_hidden * slope_s[:, at]
        ).astype(jnp.bfloat16)

    d_w[...] = (grad[z * 2 + core] + grad_in[z]) * scale
    for step in range(1, n_z):
        sends[step - 1].wait_recv()
        tall = part_in[step].astype(jnp.float32)
        d_w[...] += jnp.concatenate(
            [tall[i * piece:(i + 1) * piece, :] for i in range(cols)], axis=1
        )
    for copy in cots + hids + ws + pairs + relays + sends:
        copy.wait_send()


def kernel_body(n_zero, n_data, pre_acts, cotangent, w_out):
    tokens, width = cotangent.shape
    own_rows = w_out.shape[0]
    ffh = own_rows * n_zero
    piece = own_rows // n_data
    n_z = n_data // 2
    tall = -(-(width // LANES * piece) // 16) * 16
    scale = 1.0 / math.sqrt(tokens * n_data * n_zero)
    dma = pltpu.SemaphoreType.DMA
    d_pre, d_w = pl.pallas_call(
        functools.partial(kernel, n_zero, n_data, scale),
        out_shape=(
            jax.ShapeDtypeStruct((tokens, 2 * ffh), jnp.bfloat16),
            jax.ShapeDtypeStruct((piece, width), jnp.float32),
        ),
        in_specs=[pl.BlockSpec(memory_space=pl.ANY)] * 3,
        out_specs=(pl.BlockSpec(memory_space=pltpu.VMEM),) * 2,
        scratch_shapes=[
            pltpu.VMEM((tokens, 2 * ffh), jnp.bfloat16),
            pltpu.VMEM((n_zero, tokens, width), jnp.bfloat16),
            pltpu.VMEM((ffh, width), jnp.bfloat16),
            pltpu.VMEM((tokens, ffh), jnp.float32),
            pltpu.VMEM((tokens, ffh), jnp.float32),
            pltpu.VMEM((ffh, tokens), jnp.bfloat16),
            pltpu.VMEM((n_zero, own_rows, tokens), jnp.bfloat16),
            pltpu.VMEM((n_data, piece, width), jnp.float32),
            pltpu.VMEM((n_z, piece, width), jnp.float32),
            pltpu.VMEM((n_z, tall, LANES), jnp.bfloat16),
            pltpu.VMEM((n_z, tall, LANES), jnp.bfloat16),
            dma((3,)),
            dma((n_zero,)), dma((n_zero,)),
            dma((n_zero,)), dma((n_zero,)),
            dma((n_zero,)), dma((n_zero,)),
            dma((n_zero,)), dma((n_zero,)),
            dma((n_z,)), dma((n_z,)),
            dma((n_z,)), dma((n_z,)),
        ],
        compiler_params=pltpu.CompilerParams(
            collective_id=0, has_side_effects=True, vmem_limit_bytes=40 * 1024 * 1024
        ),
    )(pre_acts, cotangent, w_out)
    return d_pre, d_w.reshape(1, piece * width)


def solution(mesh):
    n_zero, n_data = mesh.shape["zero"], mesh.shape["dp"]

    def body(pre_acts, cotangent, w_out):
        tokens, width = cotangent.shape
        own_rows = w_out.shape[0]
        fits = (
            n_zero > 1 and n_data > 2 and n_data % 2 == 0
            and own_rows % (8 * n_data) == 0 and own_rows % 32 == 0
            and width % LANES == 0 and tokens % LANES == 0
            and (own_rows * n_zero) % (2 * LANES) == 0
        )
        if not fits:
            return general_body(pre_acts, cotangent, w_out)
        return kernel_body(n_zero, n_data, pre_acts, cotangent, w_out)

    return jax.shard_map(
        body,
        mesh=mesh,
        in_specs=(P(("dp", "zero"), None), P(("dp", "zero"), None), P("zero", None)),
        out_specs=(P(("dp", "zero"), None), P("zero", "dp")),
        check_vma=False,
    )
```

time: 162 us -> 34.9 us (0.22); the launches traced: 160 us -> 34.7 us
  waiting for transfers between devices: 133 us -> 0 us
  Pallas kernels: 0 us -> 29.5 us
  between operations: 13.8 us -> 0.65 us
  matrix products: 5.49 us -> 0 us
  local copies, waits for them, and re-layouts: 6.28 us -> 4.58 us
    unnamed x4 -> x0, waiting for transfers between devices: 56.2 us -> none
    reduce_scatter x1 -> x0, waiting for transfers between devices: 45.8 us -> none  [body(): lax.psum_scatter(jnp.einsum('th,td->hd', hidden, cotangent, preferred_ele...]
    all_gather x1 -> x0, waiting for transfers between devices: 31.2 us -> none  [body(): lax.all_gather(w_out, 'zero', axis=0, tiled=True)]
    pallas_call x0 -> x1, Pallas kernels: none -> 29.5 us  [kernel_body(): pl.pallas_call(functools.partial(kernel, n_zero, n_data, scale), out_shap...]
    dot_general x2 -> x0, matrix products: 5.49 us -> none  [the longest x1 3.41 us: body(): jnp.einsum('th,td->hd', hidden, cotangent, preferred_element_type=jnp.flo...]
    reshape x1 -> x0, local copies, waits for them, and re-layouts: 2.19 us -> none  [body(): blocks = owned.reshape(n_data, piece_len)]
  transfers between devices with their start and end apart: 3 -> 0, of which waited for: 3 -> 0; matrix products, arithmetic and copies ran while one was open for 4% -> 0% of each run, Pallas kernels for 0% -> 0%
where the time goes in v1:
time: 34.9 us; the launch traced here: 34.7 us
  Pallas kernels  29.5 us (85%)
  local copies, waits for them, and re-layouts  4.58 us (13%)
  between operations  0.65 us (2%)
    pallas_call x1, Pallas kernels, kernel_body(): pl.pallas_call(functools.partial(kernel, n_zero, n_data, scale), out_shap...  29.5 us
    unnamed x8, local copies, waits for them, and re-layouts  4.58 us

profile of v1, /device:TPU:1, one launch (start us, length us, event | category | flops | bytes accessed | tf_op | source)
XLA Modules:
  0.0 34.7 jit_solution(306654433139886951)
XLA Ops:
  0.6 0.0 copy-start
  0.6 1.1 %copy-done = bf16[128,2560]{1,0:T(8,128)(2,1)S(1)} copy-done((bf16[128,2560]{1,0:T(8,128)(2,1)S(1)}, bf16[128,2560]{1,0:T(8,128)(2,1)}, u32[]{:S(2)}) %copy-start) | copy-done | bytes 655384
  1.7 0.0 copy-start.1
  1.7 1.0 %copy-done.1 = bf16[320,640]{1,0:T(8,128)(2,1)S(1)} copy-done((bf16[320,640]{1,0:T(8,128)(2,1)S(1)}, bf16[320,640]{1,0:T(8,128)(2,1)}, u32[]{:S(2)}) %copy-start.1) | copy-done | bytes 409624
  2.7 0.0 copy-start.2
  2.7 0.9 %copy-done.2 = bf16[128,640]{1,0:T(8,128)(2,1)S(1)} copy-done((bf16[128,640]{1,0:T(8,128)(2,1)S(1)}, bf16[128,640]{1,0:T(8,128)(2,1)}, u32[]{:S(2)}) %copy-start.2) | copy-done | bytes 163864
  3.6 29.5 %shard_map.50 = (bf16[128,2560]{1,0:T(8,128)(2,1)S(1)}, f32[40,640]{1,0:T(8,128)S(1)}) custom-call(bf16[128,2560]{1,0:T(8,128)(2,1)S(1)} %copy-done, bf16[128,640]{1,0:T(8,128)(2,1)S(1)} %copy-done.2, bf16[320,640]{1,0:T(8,128)(2,1)S(1)} %copy-done.1), custom_call_target="tpu_custom_call" | custom-call | tf_op jit(solution)/shard_map/pallas_call | solution.py:223
  33.1 0.7 %copy.5 = f32[1,1,40,640]{3,1,2,0:T(1,128)} copy(f32[1,1,40,640]{3,2,1,0:T(8,128)S(1)} %bitcast.3) | data formatting | bytes 204800
  33.9 0.8 %copy.7 = bf16[128,2560]{1,0:T(8,128)(2,1)} copy(bf16[128,2560]{1,0:T(8,128)(2,1)S(1)} %get-tuple-element.8) | data formatting | bytes 1310720
Async XLA Ops:
  0.6 1.1 %copy-start = (bf16[128,2560]{1,0:T(8,128)(2,1)S(1)}, bf16[128,2560]{1,0:T(8,128)(2,1)}, u32[]{:S(2)}) copy-start(bf16[128,2560]{1,0:T(8,128)(2,1)} %pre_hbm.1) | copy-start | bytes 1966084
  1.7 1.0 %copy-start.1 = (bf16[320,640]{1,0:T(8,128)(2,1)S(1)}, bf16[320,640]{1,0:T(8,128)(2,1)}, u32[]{:S(2)}) copy-start(bf16[320,640]{1,0:T(8,128)(2,1)} %w_hbm.1) | copy-start | bytes 1228804
  2.7 0.9 %copy-start.2 = (bf16[128,640]{1,0:T(8,128)(2,1)S(1)}, bf16[128,640]{1,0:T(8,128)(2,1)}, u32[]{:S(2)}) copy-start(bf16[128,640]{1,0:T(8,128)(2,1)} %cot_hbm.1) | copy-start | bytes 491524

commit v2 on v1

--- a/solution.py
+++ b/solution.py
@@ -58,7 +58,6 @@
     tokens, width = cot_hbm.shape
     own_rows = w_hbm.shape[0]
     ffh = own_rows * n_zero
-    half = own_rows // 2
     n_z = n_data // 2
     piece = own_rows // n_data
     cols = width // LANES
@@ -67,15 +66,21 @@
     core = lax.rem(dp, 2)
     z = lax.div(dp, 2)
     twin = z * 2 + (1 - core)
-
-    def zero_at(step):
-        return lax.rem(zero + step, n_zero)
+    a = zero + 1 - 2 * lax.rem(zero, 2)
+    b = lax.rem(zero + 2, 4)
+    c = lax.rem(a + 2, 4)
 
     def z_at(step):
         return lax.rem(z + step, n_z)
 
     def rows(index, size):
         return pl.ds(pl.multiple_of(index * size, size), size)
+
+    def remote(src, dst, sems, i, group, data=dp):
+        return pltpu.make_async_remote_copy(
+            src_ref=src, dst_ref=dst, send_sem=sems[0].at[i], recv_sem=sems[1].at[i],
+            device_id=(data, group), device_id_type=MESH,
+        )
 
     into = [
         pltpu.make_async_copy(cot_hbm, cot_all.at[zero], local_sem.at[0]),
@@ -86,23 +91,31 @@
         copy.start()
 
     barrier = pltpu.get_barrier_semaphore()
-    for step in range(1, n_zero):
-        pl.semaphore_signal(barrier, inc=1, device_id=(dp, zero_at(step)), device_id_type=MESH)
+    for peer in (a, b, c):
+        pl.semaphore_signal(barrier, inc=1, device_id=(dp, peer), device_id_type=MESH)
     for step in range(1, n_z):
         pl.semaphore_signal(
             barrier, inc=1, device_id=(z_at(step) * 2 + core, zero), device_id_type=MESH
         )
     pl.semaphore_signal(barrier, inc=1, device_id=(twin, zero), device_id_type=MESH)
-    pl.semaphore_wait(barrier, n_zero - 1 + n_z - 1 + 1)
-
-    cots = []
-    for step in range(1, n_zero):
-        cots.append(pltpu.make_async_remote_copy(
-            src_ref=cot_hbm, dst_ref=cot_all.at[zero],
-            send_sem=cot_send.at[step], recv_sem=cot_recv.at[step],
-            device_id=(dp, zero_at(step)), device_id_type=MESH,
-        ))
-        cots[-1].start()
+    pl.semaphore_wait(barrier, 3 + n_z - 1 + 1)
+
+    upper, lower = pl.ds(0, tokens // 2), pl.ds(tokens // 2, tokens // 2)
+    sems = (cot_send, cot_recv)
+
+    def cot_at(peer, part_of):
+        return cot_all.at[peer, part_of, :]
+
+    cots = [
+        remote(cot_hbm.at[upper, :], cot_at(zero, upper), sems, 0, a),
+        remote(cot_hbm.at[lower, :], cot_at(zero, lower), sems, 1, b),
+        remote(cot_hbm.at[lower, :], cot_at(zero, lower), sems, 2, a),
+        remote(cot_hbm.at[upper, :], cot_at(zero, upper), sems, 3, b),
+        remote(cot_at(a, upper), cot_at(a, upper), sems, 4, b),
+        remote(cot_at(b, lower), cot_at(b, lower), sems, 5, a),
+    ]
+    for copy in cots[:4]:
+        copy.start()
 
     into[1].wait()
     for tile in range(ffh // LANES):
@@ -113,59 +126,62 @@
         act_s[:, at] = act
         slope_s[:, at] = value * slope
         hid_t[at, :] = (value * act).T.astype(jnp.bfloat16)
-    hids = []
-    for step in range(1, n_zero):
-        hids.append(pltpu.make_async_remote_copy(
-            src_ref=hid_t.at[rows(zero_at(step), own_rows), :], dst_ref=hid_all.at[zero],
-            send_sem=hid_send.at[step], recv_sem=hid_recv.at[step],
-            device_id=(dp, zero_at(step)), device_id_type=MESH,
-        ))
-        hids[-1].start()
-
-    def w_half(block, part_of):
-        return pl.ds(pl.multiple_of(block * own_rows + part_of * half, half), half)
-
-    ws = []
-    for step in range(1, n_zero):
-        ws.append(pltpu.make_async_remote_copy(
-            src_ref=w_hbm.at[w_half(0, core), :], dst_ref=w_all.at[w_half(zero, core), :],
-            send_sem=w_send.at[step], recv_sem=w_recv.at[step],
-            device_id=(dp, zero_at(step)), device_id_type=MESH,
-        ))
-        ws[-1].start()
+    hids = [
+        remote(hid_t.at[rows(peer, own_rows), :], hid_all.at[zero], (hid_send, hid_recv), i, peer)
+        for i, peer in enumerate((c, a, b))
+    ]
+    for copy in hids:
+        copy.start()
+    cots[0].wait_recv()
+    cots[4].start()
+    cots[1].wait_recv()
+    cots[5].start()
+
+    quarter = own_rows // 4
+    sems = (w_send, w_recv)
+
+    def w_quarter(ref, block, q):
+        at = block * own_rows + core * (2 * quarter) + q * quarter
+        return ref.at[pl.ds(pl.multiple_of(at, quarter), quarter), :]
+
+    ws = [
+        remote(w_quarter(w_hbm, 0, 0), w_quarter(w_all, zero, 0), sems, 0, a),
+        remote(w_quarter(w_hbm, 0, 1), w_quarter(w_all, zero, 1), sems, 1, b),
+        remote(w_quarter(w_hbm, 0, 1), w_quarter(w_all, zero, 1), sems, 2, a),
+        remote(w_quarter(w_hbm, 0, 0), w_quarter(w_all, zero, 0), sems, 3, b),
+        remote(w_quarter(w_all, a, 0), w_quarter(w_all, a, 0), sems, 4, b),
+        remote(w_quarter(w_all, b, 1), w_quarter(w_all, b, 1), sems, 5, a),
+    ]
+    for copy in ws[:4]:
+        copy.start()
 
     into[0].wait()
     grad[...] = jnp.dot(
         hid_t[rows(zero, own_rows), :], cot_all[zero], preferred_element_type=jnp.float32
     ).reshape(grad.shape)
-    for step in range(1, n_zero):
-        source = lax.rem(zero + n_zero - step, n_zero)
-        cots[step - 1].wait_recv()
-        hids[step - 1].wait_recv()
+    for hid, halves, source in (
+        (hids[1], (cots[2],), a), (hids[2], (cots[3],), b), (hids[0], (cots[4], cots[5]), c)
+    ):
+        hid.wait_recv()
+        for copy in halves:
+            copy.wait_recv()
         grad[...] += jnp.dot(
             hid_all[source], cot_all[source], preferred_element_type=jnp.float32
         ).reshape(grad.shape)
 
-    pairs = []
-    for k in range(n_z):
-        pairs.append(pltpu.make_async_remote_copy(
-            src_ref=grad.at[k * 2 + (1 - core)], dst_ref=grad_in.at[k],
-            send_sem=pair_send.at[k], recv_sem=pair_recv.at[k],
-            device_id=(twin, zero), device_id_type=MESH,
-        ))
-        pairs[-1].start()
-
-    relays = []
-    for step in range(1, n_zero):
-        source = lax.rem(zero + n_zero - step, n_zero)
-        relays.append(pltpu.make_async_remote_copy(
-            src_ref=w_all.at[w_half(source, core), :], dst_ref=w_all.at[w_half(source, core), :],
-            send_sem=relay_send.at[step], recv_sem=relay_recv.at[step],
-            device_id=(twin, zero), device_id_type=MESH,
-        ))
-
-    for k in range(n_z):
-        pairs[k].wait_recv()
+    pairs = [
+        remote(grad.at[k * 2 + (1 - core)], grad_in.at[k], (pair_send, pair_recv), k, zero, twin)
+        for k in range(n_z)
+    ]
+    for copy in pairs:
+        copy.start()
+    ws[0].wait_recv()
+    ws[4].start()
+    ws[1].wait_recv()
+    ws[5].start()
+
+    for copy in pairs:
+        copy.wait_recv()
     pad = part.shape[1] - cols * piece
     sends = []
     for step in range(1, n_z):
@@ -175,20 +191,29 @@
         if pad:
             tall.append(jnp.zeros((pad, LANES), jnp.float32))
         part[step] = jnp.concatenate(tall, axis=0).astype(jnp.bfloat16)
-        sends.append(pltpu.make_async_remote_copy(
-            src_ref=part.at[step], dst_ref=part_in.at[step],
-            send_sem=z_send.at[step], recv_sem=z_recv.at[step],
-            device_id=(owner * 2 + core, zero), device_id_type=MESH,
+        sends.append(remote(
+            part.at[step], part_in.at[step], (z_send, z_recv), step, zero, owner * 2 + core
         ))
         sends[-1].start()
 
-    for step in range(1, n_zero):
-        ws[step - 1].wait_recv()
-        relays[step - 1].start()
+    def w_half(block):
+        at = pl.ds(pl.multiple_of(block * own_rows + core * (2 * quarter), quarter), 2 * quarter)
+        return w_all.at[at, :]
+
+    relays = []
+    for i, (source, halves) in enumerate((
+        (a, (ws[2],)), (b, (ws[3],)), (c, (ws[4], ws[5]))
+    )):
+        for copy in halves:
+            copy.wait_recv()
+        relays.append(
+            remote(w_half(source), w_half(source), (relay_send, relay_recv), i, zero, twin)
+        )
+        relays[-1].start()
 
     into[2].wait()
-    for step in range(1, n_zero):
-        relays[step - 1].wait_recv()
+    for copy in relays:
+        copy.wait_recv()
     cot = cot_all[zero]
     for tile in range(ffh // (2 * LANES)):
         at = pl.ds(tile * 2 * LANES, 2 * LANES)
@@ -241,15 +266,15 @@
             pltpu.VMEM((n_z, tall, LANES), jnp.bfloat16),
             pltpu.VMEM((n_z, tall, LANES), jnp.bfloat16),
             dma((3,)),
-            dma((n_zero,)), dma((n_zero,)),
-            dma((n_zero,)), dma((n_zero,)),
-            dma((n_zero,)), dma((n_zero,)),
-            dma((n_zero,)), dma((n_zero,)),
+            dma((6,)), dma((6,)),
+            dma((3,)), dma((3,)),
+            dma((6,)), dma((6,)),
+            dma((3,)), dma((3,)),
             dma((n_z,)), dma((n_z,)),
             dma((n_z,)), dma((n_z,)),
         ],
         compiler_params=pltpu.CompilerParams(
-            collective_id=0, has_side_effects=True, vmem_limit_bytes=40 * 1024 * 1024
+            collective_id=0, has_side_effects=True, vmem_limit_bytes=60 * 1024 * 1024
         ),
     )(pre_acts, cotangent, w_out)
     return d_pre, d_w.reshape(1, piece * width)
@@ -262,8 +287,8 @@
         tokens, width = cotangent.shape
         own_rows = w_out.shape[0]
         fits = (
-            n_zero > 1 and n_data > 2 and n_data % 2 == 0
-            and own_rows % (8 * n_data) == 0 and own_rows % 32 == 0
+            n_zero == 4 and n_data > 2 and n_data % 2 == 0
+            and own_rows % (8 * n_data) == 0 and own_rows % 64 == 0
             and width % LANES == 0 and tokens % LANES == 0
             and (own_rows * n_zero) % (2 * LANES) == 0
         )

time: 34.9 us -> 31.1 us (0.89)
  Pallas kernels: 29.5 us -> 26.7 us
  local copies, waits for them, and re-layouts: 4.58 us -> 3.61 us
    pallas_call x1, Pallas kernels: 29.5 us -> 26.7 us  [kernel_body(): pl.pallas_call(functools.partial(kernel, n_zero, n_data, scale), out_shap...]
    unnamed x8 -> x2, local copies, waits for them, and re-layouts: 4.58 us -> 3.61 us
where the time goes in v2:
time: 31.1 us; the launch traced here: 30.9 us
  Pallas kernels  26.7 us (86%)
  local copies, waits for them, and re-layouts  3.61 us (12%)
  between operations  0.64 us (2%)
    pallas_call x1, Pallas kernels, kernel_body(): pl.pallas_call(functools.partial(kernel, n_zero, n_data, scale), out_shap...  26.7 us
    unnamed x2, local copies, waits for them, and re-layouts  3.61 us

profile of v2, /device:TPU:1, one launch (start us, length us, event | category | flops | bytes accessed | tf_op | source)
XLA Modules:
  0.0 30.9 jit_solution(12266130400328356478)
XLA Ops:
  0.6 26.7 %shard_map.50 = (bf16[128,2560]{1,0:T(8,128)(2,1)}, f32[40,640]{1,0:T(8,128)}) custom-call(bf16[128,2560]{1,0:T(8,128)(2,1)} %pre_hbm.1, bf16[128,640]{1,0:T(8,128)(2,1)} %cot_hbm.1, bf16[320,640]{1,0:T(8,128)(2,1)} %w_hbm.1), custom_call_target="tpu_custom_call" | custom-call | tf_op jit(solution)/shard_map/pallas_call | solution.py:248
  27.3 1.6 %copy.5 = f32[1,1,40,640]{3,1,2,0:T(1,128)} copy(f32[1,1,40,640]{3,2,1,0:T(8,128)} %bitcast.4) | data formatting | bytes 204800
  28.9 2.0 %copy.7 = bf16[128,2560]{1,0:T(8,128)(2,1)} copy(bf16[128,2560]{1,0:T(8,128)(2,1)} %get-tuple-element.8) | data formatting | bytes 1310720

commit v3 on v2

--- a/solution.py
+++ b/solution.py
@@ -245,6 +245,9 @@
     tall = -(-(width // LANES * piece) // 16) * 16
     scale = 1.0 / math.sqrt(tokens * n_data * n_zero)
     dma = pltpu.SemaphoreType.DMA
+    pre_acts, cotangent, w_out = (
+        pltpu.with_memory_space_constraint(x, pltpu.HBM) for x in (pre_acts, cotangent, w_out)
+    )
     d_pre, d_w = pl.pallas_call(
         functools.partial(kernel, n_zero, n_data, scale),
         out_shape=(
@@ -274,7 +277,7 @@
             dma((n_z,)), dma((n_z,)),
         ],
         compiler_params=pltpu.CompilerParams(
-            collective_id=0, has_side_effects=True, vmem_limit_bytes=60 * 1024 * 1024
+            collective_id=0, has_side_effects=True, vmem_limit_bytes=40 * 1024 * 1024
         ),
     )(pre_acts, cotangent, w_out)
     return d_pre, d_w.reshape(1, piece * width)

time: 31.1 us -> 28.2 us (0.907)
  local copies, waits for them, and re-layouts: 3.61 us -> 1.58 us
  Pallas kernels: 26.7 us -> 25.8 us
    unnamed x2, local copies, waits for them, and re-layouts: 3.61 us -> 1.58 us
    pallas_call x1, Pallas kernels: 26.7 us -> 25.8 us  [kernel_body(): pl.pallas_call(functools.partial(kernel, n_zero, n_data, scale), out_shap...]
where the time goes in v3:
time: 28.2 us; the launch traced here: 28 us
  Pallas kernels  25.8 us (91%)
  local copies, waits for them, and re-layouts  1.58 us (6%)
  between operations  0.64 us (2%)
    pallas_call x1, Pallas kernels, kernel_body(): pl.pallas_call(functools.partial(kernel, n_zero, n_data, scale), out_shap...  25.8 us
    unnamed x2, local copies, waits for them, and re-layouts  1.58 us

profile of v3, /device:TPU:1, one launch (start us, length us, event | category | flops | bytes accessed | tf_op | source)
XLA Modules:
  0.0 28.0 jit_solution(13265702291549729049)
XLA Ops:
  0.6 25.8 %shard_map.50 = (bf16[128,2560]{1,0:T(8,128)(2,1)S(1)}, f32[40,640]{1,0:T(8,128)S(1)}) custom-call(bf16[128,2560]{1,0:T(8,128)(2,1)} %pre_hbm.1, bf16[128,640]{1,0:T(8,128)(2,1)} %cot_hbm.1, bf16[320,640]{1,0:T(8,128)(2,1)} %w_hbm.1), custom_call_target="tpu_custom_call" | custom-call | tf_op jit(solution)/shard_map/pallas_call | solution.py:251
  26.4 0.7 %copy.5 = f32[1,1,40,640]{3,1,2,0:T(1,128)} copy(f32[1,1,40,640]{3,2,1,0:T(8,128)S(1)} %bitcast.3) | data formatting | bytes 204800
  27.2 0.8 %copy.7 = bf16[128,2560]{1,0:T(8,128)(2,1)} copy(bf16[128,2560]{1,0:T(8,128)(2,1)S(1)} %get-tuple-element.8) | data formatting | bytes 1310720

commit v4 on v3

--- a/solution.py
+++ b/solution.py
@@ -98,25 +98,6 @@
             barrier, inc=1, device_id=(z_at(step) * 2 + core, zero), device_id_type=MESH
         )
     pl.semaphore_signal(barrier, inc=1, device_id=(twin, zero), device_id_type=MESH)
-    pl.semaphore_wait(barrier, 3 + n_z - 1 + 1)
-
-    upper, lower = pl.ds(0, tokens // 2), pl.ds(tokens // 2, tokens // 2)
-    sems = (cot_send, cot_recv)
-
-    def cot_at(peer, part_of):
-        return cot_all.at[peer, part_of, :]
-
-    cots = [
-        remote(cot_hbm.at[upper, :], cot_at(zero, upper), sems, 0, a),
-        remote(cot_hbm.at[lower, :], cot_at(zero, lower), sems, 1, b),
-        remote(cot_hbm.at[lower, :], cot_at(zero, lower), sems, 2, a),
-        remote(cot_hbm.at[upper, :], cot_at(zero, upper), sems, 3, b),
-        remote(cot_at(a, upper), cot_at(a, upper), sems, 4, b),
-        remote(cot_at(b, lower), cot_at(b, lower), sems, 5, a),
-    ]
-    for copy in cots[:4]:
-        copy.start()
-
     into[1].wait()
     for tile in range(ffh // LANES):
         at = pl.ds(tile * LANES, LANES)
@@ -126,6 +107,25 @@
         act_s[:, at] = act
         slope_s[:, at] = value * slope
         hid_t[at, :] = (value * act).T.astype(jnp.bfloat16)
+    pl.semaphore_wait(barrier, 3 + n_z - 1 + 1)
+
+    upper, lower = pl.ds(0, tokens // 2), pl.ds(tokens // 2, tokens // 2)
+    sems = (cot_send, cot_recv)
+
+    def cot_at(peer, part_of):
+        return cot_all.at[peer, part_of, :]
+
+    cots = [
+        remote(cot_hbm.at[upper, :], cot_at(zero, upper), sems, 0, a),
+        remote(cot_hbm.at[lower, :], cot_at(zero, lower), sems, 1, b),
+        remote(cot_hbm.at[lower, :], cot_at(zero, lower), sems, 2, a),
+        remote(cot_hbm.at[upper, :], cot_at(zero, upper), sems, 3, b),
+        remote(cot_at(a, upper), cot_at(a, upper), sems, 4, b),
+        remote(cot_at(b, lower), cot_at(b, lower), sems, 5, a),
+    ]
+    for copy in cots[:4]:
+        copy.start()
+
     hids = [
         remote(hid_t.at[rows(peer, own_rows), :], hid_all.at[zero], (hid_send, hid_recv), i, peer)
         for i, peer in enumerate((c, a, b))
@@ -225,13 +225,15 @@
             d_hidden * slope_s[:, at]
         ).astype(jnp.bfloat16)
 
-    d_w[...] = (grad[z * 2 + core] + grad_in[z]) * scale
+    total = (grad[z * 2 + core] + grad_in[z]) * scale
     for step in range(1, n_z):
         sends[step - 1].wait_recv()
         tall = part_in[step].astype(jnp.float32)
-        d_w[...] += jnp.concatenate(
+        total += jnp.concatenate(
             [tall[i * piece:(i + 1) * piece, :] for i in range(cols)], axis=1
         )
+    for row in range(piece):
+        d_w[:, pl.ds(row * width, width)] = total[row:row + 1, :]
     for copy in cots + hids + ws + pairs + relays + sends:
         copy.wait_send()
 
@@ -252,7 +254,7 @@
         functools.partial(kernel, n_zero, n_data, scale),
         out_shape=(
             jax.ShapeDtypeStruct((tokens, 2 * ffh), jnp.bfloat16),
-            jax.ShapeDtypeStruct((piece, width), jnp.float32),
+            jax.ShapeDtypeStruct((1, piece * width), jnp.float32),
         ),
         in_specs=[pl.BlockSpec(memory_space=pl.ANY)] * 3,
         out_specs=(pl.BlockSpec(memory_space=pltpu.VMEM),) * 2,
@@ -280,7 +282,7 @@
             collective_id=0, has_side_effects=True, vmem_limit_bytes=40 * 1024 * 1024
         ),
     )(pre_acts, cotangent, w_out)
-    return d_pre, d_w.reshape(1, piece * width)
+    return d_pre, d_w
 
 
 def solution(mesh):

time: 28.2 us -> 28 us (level)
  no operation moved by 1% of the time
where the time goes in v4:
time: 28 us; the launch traced here: 27.9 us
  Pallas kernels  25.8 us (92%)
  local copies, waits for them, and re-layouts  1.48 us (5%)
  between operations  0.64 us (2%)
    pallas_call x1, Pallas kernels, kernel_body(): pl.pallas_call(functools.partial(kernel, n_zero, n_data, scale), out_shap...  25.8 us
    unnamed x2, local copies, waits for them, and re-layouts  1.48 us

profile of v4, /device:TPU:1, one launch (start us, length us, event | category | flops | bytes accessed | tf_op | source)
XLA Modules:
  0.0 27.9 jit_solution(12222179049774363348)
XLA Ops:
  0.6 25.8 %shard_map.50 = (bf16[128,2560]{1,0:T(8,128)(2,1)S(1)}, f32[1,25600]{1,0:T(1,128)S(1)}) custom-call(bf16[128,2560]{1,0:T(8,128)(2,1)} %pre_hbm.1, bf16[128,640]{1,0:T(8,128)(2,1)} %cot_hbm.1, bf16[320,640]{1,0:T(8,128)(2,1)} %w_hbm.1), custom_call_target="tpu_custom_call" | custom-call | tf_op jit(solution)/shard_map/pallas_call | solution.py:253
  26.4 0.8 %copy.7 = bf16[128,2560]{1,0:T(8,128)(2,1)} copy(bf16[128,2560]{1,0:T(8,128)(2,1)S(1)} %get-tuple-element.4) | data formatting | bytes 1310720
  27.3 0.6 %copy.8 = f32[1,25600]{1,0:T(1,128)} copy(f32[1,25600]{1,0:T(1,128)S(1)} %get-tuple-element.5) | data formatting | bytes 204800
